TPU v7x, 512 devices: a whole 4x4x16 slice. The times are simulated.
512 devices in a mesh: orb: 16 (over x_lo, y, core), grid: 32 (over z, x_hi).
Axes of the slice: x: 4 (x_hi: 2, x_lo: 2; x = x_hi * 2 + x_lo), y: 4, z: 16, core: 2. Of those that a mesh axis runs over, the one named last changes fastest.
Arguments:
- coeffs: float32 [2, 16, 262144], P(None, 'orb', 'grid'), may hold values from -6 to 6
- gvec_map: int32 [262144], P('grid'), may hold values from 0 to 65535, as said below
- projectors: float32 [2, 32, 262144], P(None, None, 'grid'), may hold values from -0.0078125 to 0.0078125
- proj_atom: int32 [32], replicated, may hold values from 0 to 7, never falling along the last dimension, each value on 1 to 8 neighbouring positions
- proj_strength: float32 [32, 32], replicated, may hold values from -96 to 96
- v_ext: float32 [128, 128, 128], P('grid'), may hold values from -6 to 6
Outputs:
- h_orbitals: float32 [2, 16, 128, 128, 128], P(None, 'orb', 'grid')
Inputs may be any that keep to these rules, and one draw needn't show every extreme that they name: `gvec_map`: entry i of each grid index's block of 8192 entries names a slot z * 512 + local column of that index, lying in slots 8 i to 8 i + 7.
All inputs are finite; a program needn't handle non-finite values.
Results may differ from a plain program's by a relative error of at most 0.0003.
Values sent between devices are 32-bit elements; how exact they have to be, the bound alone decides.
A program may use at most 128 MiB of HBM per device.

v0:
```python
import math

import jax
import jax.numpy as jnp
from jax import lax
from jax.sharding import PartitionSpec as P

HARTREE_COUPLING = 256.0
LETTERS = "abcdefgh"


def frequency(indices, grid_side):
    return jnp.where(indices < grid_side // 2, indices, indices - grid_side).astype(jnp.float32)


def dft_tables(grid_side):
    indices = jnp.arange(grid_side, dtype=jnp.int32)
    phases = indices[:, None] * indices[None, :] % grid_side
    angles = phases.astype(jnp.float32) * (2.0 * math.pi / grid_side)
    norm_scale = 1.0 / math.sqrt(grid_side)
    return (jnp.cos(angles) * norm_scale, jnp.sin(angles) * norm_scale)


def apply_axis(operand, matrix, axis_pos):
    source = LETTERS[: operand.ndim]
    target = source[:axis_pos] + "z" + source[axis_pos + 1 :]
    formula = source + "," + source[axis_pos] + "z->" + target
    return jnp.einsum(formula, operand, matrix, precision=lax.Precision.HIGHEST)


def rotate_axis(real_part, imag_part, tables, axis_pos, direction):
    cosine_table, sine_table = tables
    cos_real = apply_axis(real_part, cosine_table, axis_pos)
    sin_real = apply_axis(real_part, sine_table, axis_pos)
    cos_imag = apply_axis(imag_part, cosine_table, axis_pos)
    sin_imag = apply_axis(imag_part, sine_table, axis_pos)
    if direction > 0:
        return (cos_real - sin_imag, sin_real + cos_imag)
    return (cos_real + sin_imag, cos_imag - sin_real)


def coulomb_kernel(freq_z, freq_x, freq_y):
    squared = freq_z * freq_z + freq_x * freq_x + freq_y * freq_y
    return jnp.where(squared > 0, HARTREE_COUPLING / jnp.maximum(squared, 1.0), 0.0)


def whole_potential(density, tables, grid_place):
    grid_side = density.shape[1]
    cosine_table, sine_table = tables
    y_real = apply_axis(density, cosine_table, 2)
    y_imag = -apply_axis(density, sine_table, 2)
    x_real, x_imag = rotate_axis(y_real, y_imag, tables, 1, -1)
    exchanged = lax.all_to_all(
        jnp.stack([x_real, x_imag]), "grid", split_axis=2, concat_axis=1, tiled=True
    )
    col_width = exchanged.shape[2]
    z_real, z_imag = rotate_axis(exchanged[0], exchanged[1], tables, 0, -1)
    indices = jnp.arange(grid_side, dtype=jnp.int32)
    freq_z = frequency(indices, grid_side)[:, None, None]
    freq_x = frequency(grid_place * col_width + jnp.arange(col_width, dtype=jnp.int32), grid_side)[
        None, :, None
    ]
    freq_y = frequency(indices, grid_side)[None, None, :]
    kernel = coulomb_kernel(freq_z, freq_x, freq_y)
    back_real, back_imag = rotate_axis(z_real * kernel, z_imag * kernel, tables, 0, 1)
    returned = lax.all_to_all(
        jnp.stack([back_real, back_imag]), "grid", split_axis=1, concat_axis=2, tiled=True
    )
    u_real, u_imag = rotate_axis(returned[0], returned[1], tables, 1, 1)
    return apply_axis(u_real, cosine_table, 2) - apply_axis(u_imag, sine_table, 2)


def body(coeffs, gvec_map, projectors, proj_atom, proj_strength, v_ext):
    highest = lax.Precision.HIGHEST
    grid_side = v_ext.shape[1]
    orbitals = coeffs.shape[1]
    grid_count = lax.axis_size("grid")
    columns = grid_side * grid_side // grid_count
    grid_place = lax.axis_index("grid")
    tables = dft_tables(grid_side)
    z_freq = frequency(gvec_map // columns, grid_side)
    column = grid_place * columns + gvec_map % columns
    x_freq = frequency(column // grid_side, grid_side)
    y_freq = frequency(column % grid_side, grid_side)
    kinetic = 2.0 * (x_freq * x_freq + y_freq * y_freq + z_freq * z_freq) / (grid_side * grid_side)
    c_real, c_imag = (coeffs[0], coeffs[1])
    p_real, p_imag = (projectors[0], projectors[1])

    def inner_rows(row_data, col_data):
        return jnp.einsum("og,pg->op", row_data, col_data, precision=highest)

    partial_value = jnp.stack(
        [
            inner_rows(c_real, p_real) + inner_rows(c_imag, p_imag),
            inner_rows(c_imag, p_real) - inner_rows(c_real, p_imag),
        ]
    )
    intersection = lax.psum(partial_value, "grid")
    coupling = jnp.where(proj_atom[:, None] == proj_atom[None, :], proj_strength, 0.0)
    applied = jnp.einsum("wop,qp->woq", intersection, coupling, precision=highest)

    def spread_rows(weights, matrix):
        return jnp.dot(weights, matrix, precision=highest)

    t_real = kinetic * c_real + spread_rows(applied[0], p_real) - spread_rows(applied[1], p_imag)
    t_imag = kinetic * c_imag + spread_rows(applied[0], p_imag) + spread_rows(applied[1], p_real)

    def put_slots(values):
        flattened = (
            jnp.zeros(values.shape[:-1] + (grid_side * columns,), jnp.float32)
            .at[:, gvec_map]
            .set(values)
        )
        return flattened.reshape(values.shape[:-1] + (grid_side, columns))

    stick_real, stick_imag = rotate_axis(
        put_slots(jnp.concatenate([c_real, t_real], 0)),
        put_slots(jnp.concatenate([c_imag, t_imag], 0)),
        tables,
        1,
        1,
    )
    sticks = jnp.stack([stick_real, stick_imag])
    received = lax.all_to_all(sticks, "grid", split_axis=2, concat_axis=3, tiled=True)
    reshaped = received.reshape(received.shape[:3] + (grid_side, grid_side))
    x_real, x_imag = rotate_axis(reshaped[0], reshaped[1], tables, 2, 1)
    y_real, y_imag = rotate_axis(x_real, x_imag, tables, 3, 1)
    spaced = jnp.stack([y_real, y_imag])
    wave_space = spaced[:, :orbitals]
    term_space = spaced[:, orbitals:]
    density = lax.psum(
        jnp.sum(wave_space[0] * wave_space[0] + wave_space[1] * wave_space[1], axis=0), "orb"
    )
    hartree = whole_potential(density, tables, grid_place)
    potential = v_ext + hartree
    return term_space + potential[None, None] * wave_space


def solution(mesh):
    placed = (
        P(None, "orb", "grid"),
        P("grid"),
        P(None, None, "grid"),
        P(),
        P(),
        P("grid", None, None),
    )
    return jax.shard_map(
        body,
        mesh=mesh,
        in_specs=placed,
        out_specs=P(None, "orb", "grid", None, None),
        check_vma=False,
    )
```

profile of v0, /device:TPU:1, one launch (start us, length us, event | category | flops | bytes accessed | tf_op | source)
XLA Modules:
  0.0 517.1 jit_solution(339459350310035719)
XLA Ops:
  6.5 1.0 slice_bitcast_fusion
  7.5 2.2 convolution_bitcast_fusion.2
  9.7 2.2 convolution_bitcast_fusion
  11.9 2.2 fusion.20
  14.1 2.2 fusion.22
  16.3 70.6 %psum.14 = f32[2,32]{1,0:T(2,128)S(1)} all-reduce(f32[2,32]{1,0:T(2,128)S(1)} %bitcast.292), channel_id=1, replica_groups=mesh['orb'=16,'grid'=32] {'grid'}, use_global_device_ids=true, to_apply=%region_0.1 | all-reduce | flops 64 | bytes 512 | tf_op jit(solution)/shard_map/psum | solution.py:98
  89.8 2.7 copy.66
  92.5 34.2 %scatter_custom_fusion = f32[2,65536]{0,1:T(8,128)} fusion(s32[8192]{0:T(1024)S(1)} %add_select_fusion.5, f32[8192,2]{1,0:T(8,128)} %copy.66, f32[]{:T(128)} %constant.80.clone.1), kind=kCustom, calls=%fused_computation.4 | custom fusion | bytes 524800 | tf_op jit(solution)/shard_map/scatter | solution.py:112
  126.8 19.5 %copy.68 = f32[2,128,512]{2,1,0:T(8,128)S(1)} copy(f32[2,128,512]{0,2,1:T(8,128)} %bitcast.269) | data formatting | bytes 1048576 | tf_op jit(solution)/shard_map/reshape | solution.py:114
  146.2 0.9 fusion.93
  147.1 0.9 fusion.71
  147.9 2.7 copy.69
  150.7 34.0 %scatter_custom_fusion.1 = f32[2,65536]{0,1:T(8,128)} fusion(s32[8192]{0:T(1024)S(1)} %add_select_fusion.5, f32[8192,2]{1,0:T(8,128)} %copy.69, f32[]{:T(128)} %constant.80.clone.1), kind=kCustom, calls=%fused_computation.2 | custom fusion | bytes 524800 | tf_op jit(solution)/shard_map/scatter | solution.py:112
  184.7 19.4 %copy.71 = f32[2,128,512]{2,1,0:T(8,128)S(1)} copy(f32[2,128,512]{0,2,1:T(8,128)} %bitcast.268) | data formatting | bytes 1048576 | tf_op jit(solution)/shard_map/reshape | solution.py:114
  204.1 0.9 fusion.9
  205.0 0.9 fusion.8
  205.9 0.8 copy.76
  206.8 55.6 %all_to_all.45 = f32[2,2,128,512]{3,1,0,2:T(2,128)S(1)} all-to-all(f32[2,2,128,512]{3,1,0,2:T(2,128)S(1)} %copy.76), channel_id=1, replica_groups=mesh['orb'=16,'grid'=32] {'grid'}, dimensions={2} | all-to-all | bytes 2097152 | tf_op jit(solution)/shard_map/all_to_all | solution.py:124
  263.1 0.9 fusion.56
  264.0 0.9 fusion.99
  264.9 0.9 fusion.7
  265.7 0.8 fusion.53
  266.6 0.8 fusion.97
  267.4 0.9 fusion.6
  268.3 0.8 fusion.4
  269.1 0.8 fusion.5
  269.9 0.7 fusion.49
  270.7 138.7 %all-reduce.2.cloned.1.call-done = f32[4,128,128]{2,1,0:T(8,128)} async-done(((f32[4,128,128]{2,1,0:T(8,128)}), f32[4,128,128]{2,1,0:T(8,128)}) %all-reduce.2.cloned.1.call-update) | async-done | bytes 262160 | tf_op jit(solution)/shard_map/psum | solution.py:131
  409.4 1.6 fusion.82
  411.0 0.7 fusion.84
  411.6 1.6 convolution_negate_fusion
  413.2 0.7 fusion.78
  413.9 0.7 fusion.18
  414.5 0.7 fusion.17
  415.3 1.1 copy.86
  416.4 14.6 %all-to-all-start.1 = ((f32[2,4,128,128]{3,1,0,2:T(4,128)}), f32[2,4,128,128]{3,1,0,2:T(4,128)S(1)}, u32[]{:S(2)}, u32[]{:S(2)}) async-start(f32[2,4,128,128]{3,1,0,2:T(4,128)} %copy.86), calls=%async_computation.1 | async-start | bytes 1048576 | tf_op jit(solution)/shard_map/all_to_all | solution.py:53
  431.1 31.1 %all-to-all-done.1 = f32[2,4,128,128]{3,1,0,2:T(4,128)S(1)} async-done(((f32[2,4,128,128]{3,1,0,2:T(4,128)}), f32[2,4,128,128]{3,1,0,2:T(4,128)S(1)}, u32[]{:S(2)}, u32[]{:S(2)}) %all-to-all-start.1) | async-done | bytes 524320 | tf_op jit(solution)/shard_map/all_to_all | solution.py:53
  463.6 0.7 fusion.16
  464.3 0.7 fusion.88
  465.0 0.7 fusion.62
  465.7 0.7 fusion.15
  467.0 0.7 fusion.13
  468.1 37.0 %all_to_all.46 = f32[2,128,4,128]{3,2,0,1:T(4,128)S(1)} all-to-all(f32[2,128,4,128]{3,2,0,1:T(4,128)S(1)} %copy.96), channel_id=1, replica_groups=mesh['orb'=16,'grid'=32] {'grid'}, dimensions={1} | all-to-all | bytes 1048576 | tf_op jit(solution)/shard_map/all_to_all | solution.py:66
  505.2 0.7 fusion.59
  505.9 0.7 fusion.90
  506.5 0.7 fusion.11
  507.2 0.7 fusion.12
  509.2 0.9 fusion.44
  (41 shorter events, 7.8 us)
Async XLA Ops:
  6.5 80.5 %copy-start = (f32[2,32,8192]{2,1,0:T(8,128)S(1)}, f32[2,32,8192]{2,1,0:T(8,128)}, u32[]{:S(2)}) copy-start(f32[2,32,8192]{2,1,0:T(8,128)} %param.8) | copy-start | bytes 6291460
  6.5 80.3 %copy-start.3 = (f32[32,32]{1,0:T(8,128)S(1)}, f32[32,32]{1,0:T(8,128)}, u32[]{:S(2)}) copy-start(f32[32,32]{1,0:T(8,128)} %param.10) | copy-start | bytes 12292
  6.5 80.3 %copy-start.4 = (s32[32]{0:T(128)S(1)}, s32[32]{0:T(128)}, u32[]{:S(2)}) copy-start(s32[32]{0:T(128)} %param.9) | copy-start | bytes 388
  6.5 402.9 %all-reduce.2.cloned.1.call-start = ((), (), s32[]{:S(2)}) async-start(), calls=%async_computation.3 | async-start | bytes 524288 | tf_op jit(solution)/shard_map/psum | solution.py:131
  7.5 82.0 %copy-start.2 = (s32[8192]{0:T(1024)S(1)}, s32[8192]{0:T(1024)}, u32[]{:S(2)}) copy-start(s32[8192]{0:T(1024)} %param.7) | copy-start | bytes 98308
  416.4 45.8 %all-to-all-start.1 = ((f32[2,4,128,128]{3,1,0,2:T(4,128)}), f32[2,4,128,128]{3,1,0,2:T(4,128)S(1)}, u32[]{:S(2)}, u32[]{:S(2)}) async-start(f32[2,4,128,128]{3,1,0,2:T(4,128)} %copy.86), calls=%async_computation.1 | async-start | bytes 1048576 | tf_op jit(solution)/shard_map/all_to_all | solution.py:53
  467.7 40.8 %copy-start.1 = (f32[4,128,128]{2,1,0:T(8,128)S(1)}, f32[4,128,128]{2,1,0:T(8,128)}, u32[]{:S(2)}) copy-start(f32[4,128,128]{2,1,0:T(8,128)} %param.11) | copy-start | bytes 786436
Sparse Core Ops, SparseCore 0:
  270.8 138.5 all-reduce.1
where the time goes:
time: 523 us; the launch traced here: 517 us
  waiting for transfers between devices  170 us (33%)
  blocking collectives  163 us (31%)
  local copies, waits for them, and re-layouts  117 us (22%)
  matrix products  36.4 us (7%)
  starting transfers between devices  14.6 us (3%)
  between operations  14.1 us (3%)
    psum x1, waiting for transfers between devices, body(): lax.psum(jnp.sum(wave_space[0] * wave_space[0] + wave_space[1] * wave_spa...  139 us
    psum x1, blocking collectives, body(): intersection = lax.psum(partial_value, 'grid')  70.6 us
    scatter x2, local copies, waits for them, and re-layouts, put_slots(): flattened = jnp.zeros(values.shape[:-1] + (grid_side * columns,), jnp.flo...  68.2 us
    all_to_all x1, blocking collectives, body(): lax.all_to_all(sticks, 'grid', split_axis=2, concat_axis=3, tiled=True)  55.6 us
    reshape x2, local copies, waits for them, and re-layouts, put_slots(): return flattened.reshape(values.shape[:-1] + (grid_side, columns))  38.9 us
    all_to_all x1, blocking collectives, whole_potential(): lax.all_to_all(jnp.stack([back_real, back_imag]), 'grid', split_axis=1, c...  37 us
    all_to_all x1, waiting for transfers between devices, whole_potential(): lax.all_to_all(jnp.stack([x_real, x_imag]), 'grid', split_axis=2, concat_...  31.1 us
    dot_general x32, matrix products, apply_axis(): return jnp.einsum(formula, operand, matrix, precision=lax.Precision.HIGHEST)  25.1 us
  transfers between devices with their start and end apart: 2, of which 2 were waited for; matrix products, arithmetic and copies ran while one was open for 0% of the time, Pallas kernels for 0%

commit v1 on v0

v1 whole, which is shorter than its diff:
```python
import functools

import jax
import jax.numpy as jnp
import ml_dtypes
import numpy as np
from jax import lax
from jax.experimental import pallas as pl
from jax.experimental.pallas import tpu as pltpu
from jax.sharding import PartitionSpec as P

HARTREE_COUPLING = 256.0
F32, BF16 = jnp.float32, jnp.bfloat16
MESH = pl.DeviceIdType.MESH
HIGHEST = lax.Precision.HIGHEST
PLANES = 4
ROWS = 8
TERM_AT = {"dens": (0,), "col": (1, 2), "pot": (3,)}


def halves(table):
    high = table.astype(ml_dtypes.bfloat16)
    low = (table - high.astype(np.float64)).astype(ml_dtypes.bfloat16)
    return np.stack([high, low])


def tables(side):
    grid = side // PLANES
    place = np.arange(side)

    def turn(first, second):
        angles = 2.0 * np.pi * ((first[:, None] * second[None, :]) % side) / side
        return np.cos(angles) / np.sqrt(side), np.sin(angles) / np.sqrt(side)

    expand = (np.arange(ROWS * side)[None, :] // ROWS == place[:, None]).astype(ml_dtypes.bfloat16)
    out_z = (PLANES * np.arange(grid)[None, :] + np.arange(PLANES)[:, None]).reshape(-1)
    in_z = (2 * np.arange(side // 2)[None, :] + np.arange(2)[:, None]).reshape(-1)
    cosine, sine = turn(out_z, in_z)
    z_table = np.block([[cosine, -sine], [sine, cosine]])
    cosine, sine = turn(place, place)
    y_table = np.block([[cosine, sine], [-sine, cosine]])
    cosine, sine = [t.reshape(side, grid, 1, PLANES) for t in turn(place, place)]
    x_table = np.concatenate(
        [np.concatenate([cosine, -sine], 2), np.concatenate([sine, cosine], 2)], 0
    ).reshape(2 * side, 2 * side)
    freq = (place + 1) // 2
    angles = 2.0 * np.pi * ((place[:, None] * freq[None, :]) % side) / side
    basis = np.where(place[None, :] % 2 == 1, np.cos(angles), np.sin(angles)) * np.sqrt(2.0 / side)
    basis[:, 0] = 1.0 / np.sqrt(side)
    basis[:, side - 1] = np.where(place % 2 == 0, 1.0, -1.0) / np.sqrt(side)
    spread = np.zeros((grid, ROWS, side))
    spread[:, :PLANES] = basis.reshape(grid, PLANES, side)
    spread = spread.reshape(grid * ROWS, side)
    real = np.concatenate([halves(basis), halves(basis.T)])
    return (
        expand,
        np.concatenate([halves(z_table), halves(y_table), halves(x_table)]),
        real,
        halves(spread.T),
        halves(spread),
    )


def split(values):
    high = values.astype(BF16)
    return high, (values - high.astype(F32)).astype(BF16)


def dot(left, right):
    return jnp.dot(left, right, preferred_element_type=F32)


def left_dot(table, first, values):
    high, low = split(values)
    return dot(table[first], high) + (dot(table[first], low) + dot(table[first + 1], high))


def right_dot(values, table, first):
    high, low = split(values)
    return dot(high, table[first]) + (dot(low, table[first]) + dot(high, table[first + 1]))


def turned_dot(left, right):
    return lax.dot_general(
        left, right, (((1,), (1,)), ((), ())), precision=HIGHEST, preferred_element_type=F32
    )


def kernel(
    side, grid, orbs,
    coef_hbm, gvec_hbm, atom_hbm, strength_hbm, expand_hbm, turn_hbm, real_hbm, zf_hbm, zb_hbm, proj_hbm, vext_hbm,
    out,
    coef, gvec, atom, strength, expand, turn, real, zfor, zback, proj, vext, proj_high, proj_low,
    mask, msg_c, msg_t, got_c, got_t, wave, dens_out, dens_in, col_out, col_in, ret_out, ret_in,
    pot_out, pot_in, dot_out, dot_in, nonlocal_rows,
    in_sem, send_c, recv_c, send_t, recv_t, send_dot, recv_dot, send_dens, recv_dens,
    send_col, recv_col, send_ret, recv_ret, send_pot, recv_pot,
):
    orb, place = lax.axis_index("orb"), lax.axis_index("grid")
    nproj = strength.shape[0]
    half = side // 2
    chunks, per = recv_c.shape[0], PLANES // recv_c.shape[0]
    term_chunks = recv_t.shape[0]

    loads = []
    for index, (source, target) in enumerate(
        [(gvec_hbm, gvec), (expand_hbm, expand), (coef_hbm, coef), (turn_hbm, turn), (proj_hbm, proj),
         (atom_hbm, atom), (strength_hbm, strength), (real_hbm, real), (zf_hbm, zfor), (zb_hbm, zback),
         (vext_hbm, vext)]
    ):
        loads.append(pltpu.make_async_copy(source, target, in_sem.at[index]))
        loads[-1].start()

    def over_grid(action):
        def step(k, carry):
            hop = jnp.where(k % 2 == 1, (k + 1) // 2, grid - k // 2)
            action(lax.rem(place + hop, grid))
            return carry

        lax.fori_loop(1, grid, step, 0)

    def over_orbs(action):
        def step(k, carry):
            action(lax.rem(orb + k, orbs))
            return carry

        lax.fori_loop(1, orbs, step, 0)

    def tile(index):
        return pl.ds(pl.multiple_of(index * ROWS, ROWS), ROWS)

    def push(source, target, send_sem, recv_sem, device):
        pltpu.make_async_remote_copy(
            src_ref=source, dst_ref=target, send_sem=send_sem, recv_sem=recv_sem,
            device_id=device, device_id_type=MESH,
        ).start()

    def settle(ref, sem):
        pltpu.make_async_copy(ref, ref, sem).wait()

    barrier = pltpu.get_barrier_semaphore()

    def greet(device):
        pl.semaphore_signal(barrier, inc=1, device_id=device, device_id_type=MESH)

    over_grid(lambda other: greet((orb, other)))
    over_orbs(lambda other: greet((other, place)))

    loads[0].wait()
    slot = gvec[...]
    iz, column = slot // (PLANES * side), slot % (PLANES * side)
    ix, iy = place * PLANES + column // side, column % side

    def frequency(index):
        return jnp.where(index < half, index, index - side).astype(F32)

    fx, fy, fz = frequency(ix), frequency(iy), frequency(iz)
    kinetic = 2.0 * (fx * fx + fy * fy + fz * fz) / (side * side)

    loads[1].wait()
    offset = (slot % ROWS).astype(F32).astype(BF16)
    wide_offset = dot(offset, expand[...])
    lane = lax.broadcasted_iota(jnp.int32, (half, ROWS * side), 1)
    mask[...] = jnp.where(wide_offset == (lane % ROWS).astype(F32), 1.0, 0.0)

    def fill_messages(real_part, imag_part, target):
        real_high, real_low = split(real_part)
        imag_high, imag_low = split(imag_part)
        wide = dot(jnp.concatenate([real_high, imag_high, real_low, imag_low], 0), expand[...])

        def slots(index):
            block = (wide[index * half:(index + 1) * half] * mask[...]).astype(BF16)
            return jnp.concatenate([block[:, : PLANES * side], block[:, PLANES * side:]], 0)

        high = jnp.concatenate([slots(0), slots(1)], 0)
        low = jnp.concatenate([slots(2), slots(3)], 0)
        sticks = dot(turn[0], high) + (dot(turn[0], low) + dot(turn[1], high))
        for x in range(PLANES):
            cols = slice(x * side, (x + 1) * side)
            lines = jnp.concatenate([sticks[:side, cols], sticks[side:, cols]], 1)
            lines = right_dot(lines, turn, 2)
            for plane in range(PLANES):
                for part in range(2):
                    target[plane, pl.ds(part * PLANES + x, grid, stride=ROWS), :] = lines[
                        plane * grid:(plane + 1) * grid, part * side:(part + 1) * side
                    ]

    loads[2].wait()
    loads[3].wait()
    fill_messages(coef[0], coef[1], msg_c)

    def send_planes(msg, got, chunk, send_sem, recv_sem):
        per = PLANES // send_sem.shape[0]
        planes = pl.ds(chunk * per, per)
        over_grid(
            lambda other: push(
                msg.at[planes, tile(other), :], got.at[planes, tile(place), :],
                send_sem.at[chunk], recv_sem.at[chunk], (orb, other),
            )
        )
        got[planes, tile(place), :] = msg[planes, tile(place), :]

    def all_but_one(ref, chunk, chunks):
        per = PLANES // chunks
        return ref.at[pl.ds(chunk * per, per), pl.ds(0, (grid - 1) * ROWS), :]

    pl.semaphore_wait(barrier, grid + orbs - 2)
    send_planes(msg_c, got_c, 0, send_c, recv_c)

    loads[4].wait()

    def gather(row, carry):
        over_real, over_imag = carry
        cols = pl.ds(pl.multiple_of(row * side, side), side)
        c_real, c_imag = coef[0, pl.ds(row, 1), :], coef[1, pl.ds(row, 1), :]
        p_real, p_imag = proj[:nproj, cols], proj[nproj:, cols]
        return (
            over_real + (c_real * p_real + c_imag * p_imag),
            over_imag + (c_imag * p_real - c_real * p_imag),
        )

    zeros = jnp.zeros((nproj, side), F32)
    over_real, over_imag = lax.fori_loop(0, half, gather, (zeros, zeros), unroll=4)
    ones = jnp.ones((ROWS, side), F32)
    dot_out[...] = jnp.zeros_like(dot_out)
    dot_out[0:1, 0:nproj] = turned_dot(ones, over_real)[0:1]
    dot_out[1:2, 0:nproj] = turned_dot(ones, over_imag)[0:1]
    power = jnp.sum(coef[0] * coef[0] + coef[1] * coef[1], axis=0, keepdims=True)
    dot_out[0:1, nproj:nproj + 1] = jnp.sum(power, axis=1, keepdims=True)
    over_grid(
        lambda other: push(dot_out, dot_in.at[place], send_dot, recv_dot, (orb, other))
    )
    dot_in[place] = dot_out[...]
    for chunk in range(1, chunks):
        send_planes(msg_c, got_c, chunk, send_c, recv_c)

    def halve(block, carry):
        cols = pl.ds(pl.multiple_of(block * ROWS * side, ROWS * side), ROWS * side)
        high, low = split(proj[:, cols])
        proj_high[:, cols] = high
        proj_low[:, cols] = low
        return carry

    lax.fori_loop(0, half // ROWS, halve, 0)

    loads[5].wait()
    loads[6].wait()
    settle(dot_in.at[pl.ds(0, grid - 1)], recv_dot)
    total = jnp.sum(dot_in[...], axis=0)
    mean = total[0:1, nproj:nproj + 1] / (side * side * side)
    row = lax.broadcasted_iota(jnp.int32, (ROWS, nproj), 0)
    both = jnp.where(row == 0, total[0:1, :nproj], total[1:2, :nproj])
    owner = jnp.broadcast_to(atom[...].astype(F32), (nproj, nproj))
    coupling = jnp.where(owner == owner.T, strength[...], 0.0)
    applied_high, applied_low = split(turned_dot(both, coupling))

    def spread(first):
        high, low = proj_high[first:first + nproj], proj_low[first:first + nproj]
        return dot(applied_high, high) + (dot(applied_high, low) + dot(applied_low, high))

    on_real, on_imag = spread(0), spread(nproj)
    term_real = on_real[0:1] - on_imag[1:2]
    term_imag = on_imag[0:1] + on_real[1:2]
    for r in range(half):
        nonlocal_rows[0, r:r + 1, :] = term_real[:, r * side:(r + 1) * side]
        nonlocal_rows[1, r:r + 1, :] = term_imag[:, r * side:(r + 1) * side]
    fill_messages(
        kinetic * coef[0] + nonlocal_rows[0], kinetic * coef[1] + nonlocal_rows[1], msg_t
    )

    def send_term(moment):
        for chunk in TERM_AT.get(moment, ()):
            send_planes(msg_t, got_t, chunk, send_t, recv_t)

    for index in (7, 8, 9, 10):
        loads[index].wait()
    for chunk in range(chunks):
        planes = range(chunk * per, (chunk + 1) * per)
        settle(all_but_one(got_c, chunk, chunks), recv_c.at[chunk])
        send_term("wave%d" % chunk)
        field = left_dot(turn, 4, jnp.concatenate([got_c[p] for p in planes], 1))
        density = field[:side] * field[:side] + field[side:] * field[side:] - mean
        for k, p in enumerate(planes):
            wave[0, p] = field[:side, k * side:(k + 1) * side]
            wave[1, p] = field[side:, k * side:(k + 1) * side]
        lines = jnp.concatenate([density[:, k * side:(k + 1) * side] for k in range(per)], 0)
        lines = right_dot(lines, real, 0)
        lines = jnp.concatenate([lines[k * side:(k + 1) * side] for k in range(per)], 1)
        modes = left_dot(real, 2, lines)
        for k, p in enumerate(planes):
            dens_out[p] = modes[:, k * side:(k + 1) * side]
        span = pl.ds(chunk * per, per)
        over_orbs(
            lambda other: push(
                dens_out.at[span, tile(other), :], dens_in.at[span, tile(orb), :],
                send_dens.at[chunk], recv_dens.at[chunk], (other, place),
            )
        )
        dens_in[span, tile(orb), :] = dens_out[span, tile(orb), :]

    send_term("dens")

    stride = grid // ROWS
    shift = lax.rem(orb, stride)
    my_row = place // stride
    is_owner = lax.rem(place, stride) == shift

    col_out[...] = jnp.zeros_like(col_out)
    for chunk in range(chunks):
        span = pl.ds(chunk * per, per)
        settle(dens_in.at[span, pl.ds(0, (orbs - 1) * ROWS), :], recv_dens.at[chunk])
        for p in range(chunk * per, (chunk + 1) * per):
            summed = dens_in[p, 0:ROWS, :]
            for o in range(1, orbs):
                summed = summed + dens_in[p, o * ROWS:(o + 1) * ROWS, :]
            col_out[pl.ds(p, ROWS, stride=ROWS), :] = summed

    def send_column(row_index, carry):
        target = row_index * stride + shift

        @pl.when(target != place)
        def _():
            push(
                col_out.at[tile(row_index), :], col_in.at[tile(place), :],
                send_col, recv_col, (orb, target),
            )

        return carry

    lax.fori_loop(0, ROWS, send_column, 0)
    send_term("col")

    @pl.when(is_owner)
    def _():
        col_in[tile(place), :] = col_out[tile(my_row), :]
        settle(col_in.at[pl.ds(0, (grid - 1) * ROWS), :], recv_col)
        kx = (orb * ROWS + my_row + 1) // 2
        kz = (lax.broadcasted_iota(jnp.int32, (side, side), 0) + 1) // 2
        ky = (lax.broadcasted_iota(jnp.int32, (side, side), 1) + 1) // 2
        squared = (kx * kx + ky * ky + kz * kz).astype(F32)
        coulomb = jnp.where(squared > 0, HARTREE_COUPLING / jnp.maximum(squared, 1.0), 0.0)
        spectrum = left_dot(zfor, 0, col_in[...]) * coulomb
        ret_out[...] = left_dot(zback, 0, spectrum)
        over_grid(
            lambda other: push(
                ret_out.at[tile(other), :], ret_in.at[tile(my_row), :],
                send_ret, recv_ret, (orb, other),
            )
        )
        ret_in[tile(my_row), :] = ret_out[tile(place), :]
        settle(ret_in.at[pl.ds(0, (ROWS - 1) * ROWS), :], recv_ret)
        settle(ret_out.at[pl.ds(0, (grid - 1) * ROWS), :], send_ret)
        settle(col_out.at[pl.ds(0, (ROWS - 1) * ROWS), :], send_col)

    @pl.when(jnp.logical_not(is_owner))
    def _():
        settle(ret_in, recv_ret)
        settle(col_out, send_col)

    for p in range(PLANES):
        pot_out[p] = ret_in[pl.ds(p, ROWS, stride=ROWS), :]
    over_orbs(
        lambda other: push(
            pot_out, pot_in.at[:, tile(orb), :], send_pot, recv_pot, (other, place)
        )
    )
    pot_in[:, tile(orb), :] = pot_out[...]
    send_term("pot")

    per_term = PLANES // term_chunks
    for chunk in range(term_chunks):
        planes = range(chunk * per_term, (chunk + 1) * per_term)
        settle(all_but_one(got_t, chunk, term_chunks), recv_t.at[chunk])
        field = left_dot(turn, 4, jnp.concatenate([got_t[p] for p in planes], 1))
        for k, p in enumerate(planes):
            out[0, 0, p] = field[:side, k * side:(k + 1) * side]
            out[1, 0, p] = field[side:, k * side:(k + 1) * side]

    settle(pot_in.at[:, pl.ds(0, (orbs - 1) * ROWS), :], recv_pot)
    lines = left_dot(real, 0, jnp.concatenate([pot_in[p] for p in range(PLANES)], 1))
    lines = jnp.concatenate([lines[:, p * side:(p + 1) * side] for p in range(PLANES)], 0)
    hartree = right_dot(lines, real, 2)
    for p in range(PLANES):
        potential = vext[p] + hartree[p * side:(p + 1) * side]
        out[0, 0, p] = out[0, 0, p] + potential * wave[0, p]
        out[1, 0, p] = out[1, 0, p] + potential * wave[1, p]

    for chunk in range(chunks):
        settle(all_but_one(msg_c, chunk, chunks), send_c.at[chunk])
        span = pl.ds(chunk * per, per)
        settle(dens_out.at[span, pl.ds(0, (orbs - 1) * ROWS), :], send_dens.at[chunk])
    for chunk in range(term_chunks):
        settle(all_but_one(msg_t, chunk, term_chunks), send_t.at[chunk])
    settle(dot_in.at[pl.ds(0, grid - 1)], send_dot)
    settle(pot_in.at[:, pl.ds(0, (orbs - 1) * ROWS), :], send_pot)


def body(grid, orbs, coeffs, gvec_map, projectors, proj_atom, proj_strength, v_ext):
    side = v_ext.shape[1]
    nproj = proj_strength.shape[0]
    count = coeffs.shape[2]
    chunks, term_chunks = 2, 4
    consts = [jnp.asarray(t) for t in tables(side)]
    dma = pltpu.SemaphoreType.DMA

    def vmem(*shape, dtype=F32):
        return pltpu.VMEM(shape, dtype)

    return pl.pallas_call(
        functools.partial(kernel, side, grid, orbs),
        out_shape=jax.ShapeDtypeStruct((2, 1) + v_ext.shape, F32),
        in_specs=[pl.BlockSpec(memory_space=pltpu.HBM)] * 11,
        out_specs=pl.BlockSpec(memory_space=pltpu.VMEM),
        scratch_shapes=[
            vmem(2, side // 2, side),
            vmem(side // 2, side, dtype=jnp.int32),
            vmem(1, nproj, dtype=jnp.int32),
            vmem(nproj, nproj),
        ]
        + [pltpu.VMEM(t.shape, t.dtype) for t in consts]
        + [
            vmem(2 * nproj, count),
            vmem(*v_ext.shape),
            vmem(2 * nproj, count, dtype=BF16),
            vmem(2 * nproj, count, dtype=BF16),
            vmem(side // 2, ROWS * side),
        ]
        + [vmem(PLANES, grid * ROWS, side)] * 4
        + [
            vmem(2, PLANES, side, side),
            vmem(PLANES, side, side),
            vmem(PLANES, side, side),
            vmem(ROWS * ROWS, side),
            vmem(grid * ROWS, side),
            vmem(grid * ROWS, side),
            vmem(ROWS * ROWS, side),
            vmem(PLANES, ROWS, side),
            vmem(PLANES, side, side),
            vmem(2, 128),
            vmem(grid, 2, 128),
            vmem(2, side // 2, side),
            dma((11,)),
            dma((chunks,)), dma((chunks,)), dma((term_chunks,)), dma((term_chunks,)),
            dma, dma,
            dma((chunks,)), dma((chunks,)),
            dma, dma, dma, dma, dma, dma,
        ],
        compiler_params=pltpu.CompilerParams(
            collective_id=0, has_side_effects=True, vmem_limit_bytes=60 << 20
        ),
        name="hamiltonian",
    )(
        coeffs.reshape(2, side // 2, side),
        gvec_map.reshape(side // 2, side),
        proj_atom.reshape(1, nproj),
        proj_strength,
        *consts,
        projectors.reshape(2 * nproj, count),
        v_ext,
    )


def solution(mesh):
    placed = (
        P(None, "orb", "grid"),
        P("grid"),
        P(None, None, "grid"),
        P(),
        P(),
        P("grid", None, None),
    )
    return jax.shard_map(
        functools.partial(body, mesh.shape["grid"], mesh.shape["orb"]),
        mesh=mesh,
        in_specs=placed,
        out_specs=P(None, "orb", "grid", None, None),
        check_vma=False,
    )
```

time: 523 us -> 89.1 us (0.17)
  the two profiles are of different devices: /device:TPU:1 before, /device:TPU:40 now
where the time goes in v1:
time: 89.1 us; the launch traced here: 88.9 us
  Pallas kernels  87 us (98%)
  local copies, waits for them, and re-layouts  1.87 us (2%)
    pallas_call x1, Pallas kernels, body(): pl.pallas_call(functools.partial(kernel, side, grid, orbs), out_shape=jax...  87 us
    unnamed x1, local copies, waits for them, and re-layouts  1.87 us

profile of v1, /device:TPU:40, one launch (start us, length us, event | category | flops | bytes accessed | tf_op | source)
XLA Modules:
  0.0 88.9 jit_solution(4692097520828195883)
XLA Ops:
  0.0 87.0 %hamiltonian.1 = f32[2,1,4,128,128]{4,3,2,1,0:T(8,128)} custom-call(f32[2,64,128]{2,1,0:T(8,128)} %bitcast.5, s32[64,128]{1,0:T(8,128)} %bitcast.6, s32[1,32]{1,0:T(1,128)} %bitcast.7, f32[32,32]{1,0:T(8,128)} %strength_hbm.1, bf16[128,1024]{1,0:T(8,128)(2,1)} %constant.10.clone.expand_hbm, bf16[6,256,256]{2,1,0:T(8,128)(2,1)} %constant.11.clone.turn_hbm, ...), custom_call_target="tpu_custom_call" | custom-call | tf_op jit(solution)/shard_map/hamiltonian/pallas_call | solution.py:409
  87.0 1.9 %copy.13 = f32[2,1,4,128,128]{4,3,2,1,0:T(8,128)} copy(f32[2,1,4,128,128]{4,3,2,1,0:T(8,128)} %hamiltonian.1) | data formatting | bytes 1048576

commit v2 on v1

--- a/solution.py
+++ b/solution.py
@@ -15,7 +15,7 @@
 HIGHEST = lax.Precision.HIGHEST
 PLANES = 4
 ROWS = 8
-TERM_AT = {"dens": (0,), "col": (1, 2), "pot": (3,)}
+TERM_AT = {"dens": (0,), "col": (1,), "ret": (2, 3)}
 
 
 def halves(table):
@@ -113,7 +113,8 @@
 
     def over_grid(action):
         def step(k, carry):
-            hop = jnp.where(k % 2 == 1, (k + 1) // 2, grid - k // 2)
+            m = grid - k
+            hop = jnp.where(m % 2 == 1, (m + 1) // 2, grid - m // 2)
             action(lax.rem(place + hop, grid))
             return carry
 
@@ -204,9 +205,6 @@
         per = PLANES // chunks
         return ref.at[pl.ds(chunk * per, per), pl.ds(0, (grid - 1) * ROWS), :]
 
-    pl.semaphore_wait(barrier, grid + orbs - 2)
-    send_planes(msg_c, got_c, 0, send_c, recv_c)
-
     loads[4].wait()
 
     def gather(row, carry):
@@ -227,11 +225,12 @@
     dot_out[1:2, 0:nproj] = turned_dot(ones, over_imag)[0:1]
     power = jnp.sum(coef[0] * coef[0] + coef[1] * coef[1], axis=0, keepdims=True)
     dot_out[0:1, nproj:nproj + 1] = jnp.sum(power, axis=1, keepdims=True)
+    pl.semaphore_wait(barrier, grid + orbs - 2)
     over_grid(
         lambda other: push(dot_out, dot_in.at[place], send_dot, recv_dot, (orb, other))
     )
     dot_in[place] = dot_out[...]
-    for chunk in range(1, chunks):
+    for chunk in range(chunks):
         send_planes(msg_c, got_c, chunk, send_c, recv_c)
 
     def halve(block, carry):
@@ -283,10 +282,7 @@
         for k, p in enumerate(planes):
             wave[0, p] = field[:side, k * side:(k + 1) * side]
             wave[1, p] = field[side:, k * side:(k + 1) * side]
-        lines = jnp.concatenate([density[:, k * side:(k + 1) * side] for k in range(per)], 0)
-        lines = right_dot(lines, real, 0)
-        lines = jnp.concatenate([lines[k * side:(k + 1) * side] for k in range(per)], 1)
-        modes = left_dot(real, 2, lines)
+        modes = left_dot(real, 2, density)
         for k, p in enumerate(planes):
             dens_out[p] = modes[:, k * side:(k + 1) * side]
         span = pl.ds(chunk * per, per)
@@ -306,6 +302,7 @@
     is_owner = lax.rem(place, stride) == shift
 
     col_out[...] = jnp.zeros_like(col_out)
+    sums = []
     for chunk in range(chunks):
         span = pl.ds(chunk * per, per)
         settle(dens_in.at[span, pl.ds(0, (orbs - 1) * ROWS), :], recv_dens.at[chunk])
@@ -313,7 +310,10 @@
             summed = dens_in[p, 0:ROWS, :]
             for o in range(1, orbs):
                 summed = summed + dens_in[p, o * ROWS:(o + 1) * ROWS, :]
-            col_out[pl.ds(p, ROWS, stride=ROWS), :] = summed
+            sums.append(summed)
+    modes = right_dot(jnp.concatenate(sums, 0), real, 0)
+    for p in range(PLANES):
+        col_out[pl.ds(p, ROWS, stride=ROWS), :] = modes[p * ROWS:(p + 1) * ROWS]
 
     def send_column(row_index, carry):
         target = row_index * stride + shift
@@ -348,17 +348,21 @@
             )
         )
         ret_in[tile(my_row), :] = ret_out[tile(place), :]
+        send_term("ret")
         settle(ret_in.at[pl.ds(0, (ROWS - 1) * ROWS), :], recv_ret)
         settle(ret_out.at[pl.ds(0, (grid - 1) * ROWS), :], send_ret)
         settle(col_out.at[pl.ds(0, (ROWS - 1) * ROWS), :], send_col)
 
     @pl.when(jnp.logical_not(is_owner))
     def _():
+        send_term("ret")
         settle(ret_in, recv_ret)
         settle(col_out, send_col)
 
+    rows = jnp.concatenate([ret_in[pl.ds(p, ROWS, stride=ROWS), :] for p in range(PLANES)], 0)
+    rows = right_dot(rows, real, 2)
     for p in range(PLANES):
-        pot_out[p] = ret_in[pl.ds(p, ROWS, stride=ROWS), :]
+        pot_out[p] = rows[p * ROWS:(p + 1) * ROWS]
     over_orbs(
         lambda other: push(
             pot_out, pot_in.at[:, tile(orb), :], send_pot, recv_pot, (other, place)
@@ -377,11 +381,9 @@
             out[1, 0, p] = field[side:, k * side:(k + 1) * side]
 
     settle(pot_in.at[:, pl.ds(0, (orbs - 1) * ROWS), :], recv_pot)
-    lines = left_dot(real, 0, jnp.concatenate([pot_in[p] for p in range(PLANES)], 1))
-    lines = jnp.concatenate([lines[:, p * side:(p + 1) * side] for p in range(PLANES)], 0)
-    hartree = right_dot(lines, real, 2)
+    hartree = left_dot(real, 0, jnp.concatenate([pot_in[p] for p in range(PLANES)], 1))
     for p in range(PLANES):
-        potential = vext[p] + hartree[p * side:(p + 1) * side]
+        potential = vext[p] + hartree[:, p * side:(p + 1) * side]
         out[0, 0, p] = out[0, 0, p] + potential * wave[0, p]
         out[1, 0, p] = out[1, 0, p] + potential * wave[1, p]
 

time: 89.1 us -> 79.7 us (0.89)
  the two profiles are of different devices: /device:TPU:40 before, /device:TPU:1 now
where the time goes in v2:
time: 79.7 us; the launch traced here: 79.5 us
  Pallas kernels  77.6 us (97%)
  local copies, waits for them, and re-layouts  1.87 us (2%)
    pallas_call x1, Pallas kernels, body(): pl.pallas_call(functools.partial(kernel, side, grid, orbs), out_shape=jax...  77.6 us
    unnamed x1, local copies, waits for them, and re-layouts  1.87 us

profile of v2, /device:TPU:1, one launch (start us, length us, event | category | flops | bytes accessed | tf_op | source)
XLA Modules:
  0.0 79.5 jit_solution(6264355848144952271)
XLA Ops:
  0.0 77.6 %hamiltonian.1 = f32[2,1,4,128,128]{4,3,2,1,0:T(8,128)} custom-call(f32[2,64,128]{2,1,0:T(8,128)} %bitcast.5, s32[64,128]{1,0:T(8,128)} %bitcast.6, s32[1,32]{1,0:T(1,128)} %bitcast.7, f32[32,32]{1,0:T(8,128)} %strength_hbm.1, bf16[128,1024]{1,0:T(8,128)(2,1)} %constant.10.clone.expand_hbm, bf16[6,256,256]{2,1,0:T(8,128)(2,1)} %constant.11.clone.turn_hbm, ...), custom_call_target="tpu_custom_call" | custom-call | tf_op jit(solution)/shard_map/hamiltonian/pallas_call | solution.py:411
  77.6 1.9 %copy.13 = f32[2,1,4,128,128]{4,3,2,1,0:T(8,128)} copy(f32[2,1,4,128,128]{4,3,2,1,0:T(8,128)} %hamiltonian.1) | data formatting | bytes 1048576

commit v3 on v2

--- a/solution.py
+++ b/solution.py
@@ -15,7 +15,7 @@
 HIGHEST = lax.Precision.HIGHEST
 PLANES = 4
 ROWS = 8
-TERM_AT = {"dens": (0,), "col": (1,), "ret": (2, 3)}
+TERM_AT = {"dens": (0,), "col": (1,), "idle": (2, 3), "ret": (2, 3)}
 
 
 def halves(table):
@@ -130,6 +130,9 @@
     def tile(index):
         return pl.ds(pl.multiple_of(index * ROWS, ROWS), ROWS)
 
+    def planes_of(index):
+        return pl.ds(pl.multiple_of(index * ROWS, ROWS), PLANES)
+
     def push(source, target, send_sem, recv_sem, device):
         pltpu.make_async_remote_copy(
             src_ref=source, dst_ref=target, send_sem=send_sem, recv_sem=recv_sem,
@@ -139,6 +142,10 @@
     def settle(ref, sem):
         pltpu.make_async_copy(ref, ref, sem).wait()
 
+    def settle_rows(count, sem):
+        settle(col_in.at[pl.ds(0, count), :], sem)
+
+    col_in[...] = jnp.zeros_like(col_in)
     barrier = pltpu.get_barrier_semaphore()
 
     def greet(device):
@@ -321,7 +328,7 @@
         @pl.when(target != place)
         def _():
             push(
-                col_out.at[tile(row_index), :], col_in.at[tile(place), :],
+                col_out.at[planes_of(row_index), :], col_in.at[planes_of(place), :],
                 send_col, recv_col, (orb, target),
             )
 
@@ -333,7 +340,7 @@
     @pl.when(is_owner)
     def _():
         col_in[tile(place), :] = col_out[tile(my_row), :]
-        settle(col_in.at[pl.ds(0, (grid - 1) * ROWS), :], recv_col)
+        settle_rows((grid - 1) * PLANES, recv_col)
         kx = (orb * ROWS + my_row + 1) // 2
         kz = (lax.broadcasted_iota(jnp.int32, (side, side), 0) + 1) // 2
         ky = (lax.broadcasted_iota(jnp.int32, (side, side), 1) + 1) // 2
@@ -343,21 +350,21 @@
         ret_out[...] = left_dot(zback, 0, spectrum)
         over_grid(
             lambda other: push(
-                ret_out.at[tile(other), :], ret_in.at[tile(my_row), :],
+                ret_out.at[planes_of(other), :], ret_in.at[planes_of(my_row), :],
                 send_ret, recv_ret, (orb, other),
             )
         )
         ret_in[tile(my_row), :] = ret_out[tile(place), :]
         send_term("ret")
-        settle(ret_in.at[pl.ds(0, (ROWS - 1) * ROWS), :], recv_ret)
-        settle(ret_out.at[pl.ds(0, (grid - 1) * ROWS), :], send_ret)
-        settle(col_out.at[pl.ds(0, (ROWS - 1) * ROWS), :], send_col)
+        settle_rows((ROWS - 1) * PLANES, recv_ret)
+        settle_rows((grid - 1) * PLANES, send_ret)
+        settle_rows((ROWS - 1) * PLANES, send_col)
 
     @pl.when(jnp.logical_not(is_owner))
     def _():
-        send_term("ret")
-        settle(ret_in, recv_ret)
-        settle(col_out, send_col)
+        send_term("idle")
+        settle_rows(ROWS * PLANES, recv_ret)
+        settle_rows(ROWS * PLANES, send_col)
 
     rows = jnp.concatenate([ret_in[pl.ds(p, ROWS, stride=ROWS), :] for p in range(PLANES)], 0)
     rows = right_dot(rows, real, 2)
@@ -408,6 +415,15 @@
     def vmem(*shape, dtype=F32):
         return pltpu.VMEM(shape, dtype)
 
+    operands = [
+        coeffs.reshape(2, side // 2, side),
+        gvec_map.reshape(side // 2, side),
+        proj_atom.reshape(1, nproj),
+        proj_strength,
+        *consts,
+        projectors.reshape(2 * nproj, count),
+        v_ext,
+    ]
     return pl.pallas_call(
         functools.partial(kernel, side, grid, orbs),
         out_shape=jax.ShapeDtypeStruct((2, 1) + v_ext.shape, F32),
@@ -448,18 +464,10 @@
             dma, dma, dma, dma, dma, dma,
         ],
         compiler_params=pltpu.CompilerParams(
-            collective_id=0, has_side_effects=True, vmem_limit_bytes=60 << 20
+            collective_id=0, has_side_effects=True, vmem_limit_bytes=32 << 20
         ),
         name="hamiltonian",
-    )(
-        coeffs.reshape(2, side // 2, side),
-        gvec_map.reshape(side // 2, side),
-        proj_atom.reshape(1, nproj),
-        proj_strength,
-        *consts,
-        projectors.reshape(2 * nproj, count),
-        v_ext,
-    )
+    )(*[pltpu.with_memory_space_constraint(x, pltpu.HBM) for x in operands])
 
 
 def solution(mesh):

time: 79.7 us -> 76.2 us (0.956)
  Pallas kernels: 77.6 us -> 75.3 us
  local copies, waits for them, and re-layouts: 1.87 us -> 0.8 us
    pallas_call x1, Pallas kernels: 77.6 us -> 75.3 us  [body(): pl.pallas_call(functools.partial(kernel, side, grid, orbs), out_shape=jax...]
    unnamed x1, local copies, waits for them, and re-layouts: 1.87 us -> 0.8 us
where the time goes in v3:
time: 76.2 us; the launch traced here: 76.1 us
  Pallas kernels  75.3 us (99%)
  local copies, waits for them, and re-layouts  0.8 us (1%)
    pallas_call x1, Pallas kernels, body(): pl.pallas_call(functools.partial(kernel, side, grid, orbs), out_shape=jax...  75.3 us

profile of v3, /device:TPU:1, one launch (start us, length us, event | category | flops | bytes accessed | tf_op | source)
XLA Modules:
  0.0 76.1 jit_solution(7760883761470067881)
XLA Ops:
  0.0 75.3 %hamiltonian.1 = f32[2,1,4,128,128]{4,3,2,1,0:T(8,128)S(1)} custom-call(f32[2,64,128]{2,1,0:T(8,128)} %bitcast.5, s32[64,128]{1,0:T(8,128)} %bitcast.6, s32[1,32]{1,0:T(1,128)} %bitcast.7, f32[32,32]{1,0:T(8,128)} %strength_hbm.1, bf16[128,1024]{1,0:T(8,128)(2,1)} %constant.10.clone.expand_hbm, bf16[6,256,256]{2,1,0:T(8,128)(2,1)} %constant.11.clone.turn_hbm, ...), custom_call_target="tpu_custom_call" | custom-call | tf_op jit(solution)/shard_map/hamiltonian/pallas_call | solution.py:427
  75.3 0.8 %copy.13 = f32[2,1,4,128,128]{4,3,2,1,0:T(8,128)} copy(f32[2,1,4,128,128]{4,3,2,1,0:T(8,128)S(1)} %hamiltonian.1) | data formatting | bytes 1048576

commit v4 on v3

--- a/solution.py
+++ b/solution.py
@@ -15,6 +15,7 @@
 HIGHEST = lax.Precision.HIGHEST
 PLANES = 4
 ROWS = 8
+TERM_BEFORE = 3
 TERM_AT = {"dens": (0,), "col": (1,), "idle": (2, 3), "ret": (2, 3)}
 
 
@@ -228,10 +229,10 @@
     over_real, over_imag = lax.fori_loop(0, half, gather, (zeros, zeros), unroll=4)
     ones = jnp.ones((ROWS, side), F32)
     dot_out[...] = jnp.zeros_like(dot_out)
-    dot_out[0:1, 0:nproj] = turned_dot(ones, over_real)[0:1]
-    dot_out[1:2, 0:nproj] = turned_dot(ones, over_imag)[0:1]
-    power = jnp.sum(coef[0] * coef[0] + coef[1] * coef[1], axis=0, keepdims=True)
-    dot_out[0:1, nproj:nproj + 1] = jnp.sum(power, axis=1, keepdims=True)
+    power = coef[0] * coef[0] + coef[1] * coef[1]
+    power = jnp.sum(power.reshape(half // ROWS, ROWS, side), axis=0)
+    used = 2 * nproj + ROWS
+    dot_out[0:1, 0:used] = turned_dot(ones, jnp.concatenate([over_real, over_imag, power], 0))[0:1]
     pl.semaphore_wait(barrier, grid + orbs - 2)
     over_grid(
         lambda other: push(dot_out, dot_in.at[place], send_dot, recv_dot, (orb, other))
@@ -253,9 +254,9 @@
     loads[6].wait()
     settle(dot_in.at[pl.ds(0, grid - 1)], recv_dot)
     total = jnp.sum(dot_in[...], axis=0)
-    mean = total[0:1, nproj:nproj + 1] / (side * side * side)
+    mean = jnp.sum(total[:, 2 * nproj:used], axis=1, keepdims=True) / (side * side * side)
     row = lax.broadcasted_iota(jnp.int32, (ROWS, nproj), 0)
-    both = jnp.where(row == 0, total[0:1, :nproj], total[1:2, :nproj])
+    both = jnp.where(row == 0, total[:, :nproj], total[:, nproj:2 * nproj])
     owner = jnp.broadcast_to(atom[...].astype(F32), (nproj, nproj))
     coupling = jnp.where(owner == owner.T, strength[...], 0.0)
     applied_high, applied_low = split(turned_dot(both, coupling))
@@ -379,7 +380,8 @@
     send_term("pot")
 
     per_term = PLANES // term_chunks
-    for chunk in range(term_chunks):
+
+    def term_in_space(chunk):
         planes = range(chunk * per_term, (chunk + 1) * per_term)
         settle(all_but_one(got_t, chunk, term_chunks), recv_t.at[chunk])
         field = left_dot(turn, 4, jnp.concatenate([got_t[p] for p in planes], 1))
@@ -387,12 +389,18 @@
             out[0, 0, p] = field[:side, k * side:(k + 1) * side]
             out[1, 0, p] = field[side:, k * side:(k + 1) * side]
 
+    for chunk in range(TERM_BEFORE):
+        term_in_space(chunk)
     settle(pot_in.at[:, pl.ds(0, (orbs - 1) * ROWS), :], recv_pot)
     hartree = left_dot(real, 0, jnp.concatenate([pot_in[p] for p in range(PLANES)], 1))
     for p in range(PLANES):
-        potential = vext[p] + hartree[:, p * side:(p + 1) * side]
-        out[0, 0, p] = out[0, 0, p] + potential * wave[0, p]
-        out[1, 0, p] = out[1, 0, p] + potential * wave[1, p]
+        vext[p] = vext[p] + hartree[:, p * side:(p + 1) * side]
+    for chunk in range(term_chunks):
+        if chunk >= TERM_BEFORE:
+            term_in_space(chunk)
+        for p in range(chunk * per_term, (chunk + 1) * per_term):
+            out[0, 0, p] = out[0, 0, p] + vext[p] * wave[0, p]
+            out[1, 0, p] = out[1, 0, p] + vext[p] * wave[1, p]
 
     for chunk in range(chunks):
         settle(all_but_one(msg_c, chunk, chunks), send_c.at[chunk])
@@ -454,8 +462,8 @@
             vmem(ROWS * ROWS, side),
             vmem(PLANES, ROWS, side),
             vmem(PLANES, side, side),
-            vmem(2, 128),
-            vmem(grid, 2, 128),
+            vmem(1, 128),
+            vmem(grid, 1, 128),
             vmem(2, side // 2, side),
             dma((11,)),
             dma((chunks,)), dma((chunks,)), dma((term_chunks,)), dma((term_chunks,)),

time: 76.2 us -> 76.5 us (level)
  no operation moved by 1% of the time
where the time goes in v4:
time: 76.5 us; the launch traced here: 76.4 us
  Pallas kernels  75.6 us (99%)
  local copies, waits for them, and re-layouts  0.8 us (1%)
    pallas_call x1, Pallas kernels, body(): pl.pallas_call(functools.partial(kernel, side, grid, orbs), out_shape=jax...  75.6 us

profile of v4, /device:TPU:1, one launch (start us, length us, event | category | flops | bytes accessed | tf_op | source)
XLA Modules:
  0.0 76.4 jit_solution(4582353855809377344)
XLA Ops:
  0.0 75.6 %hamiltonian.1 = f32[2,1,4,128,128]{4,3,2,1,0:T(8,128)S(1)} custom-call(f32[2,64,128]{2,1,0:T(8,128)} %bitcast.5, s32[64,128]{1,0:T(8,128)} %bitcast.6, s32[1,32]{1,0:T(1,128)} %bitcast.7, f32[32,32]{1,0:T(8,128)} %strength_hbm.1, bf16[128,1024]{1,0:T(8,128)(2,1)} %constant.10.clone.expand_hbm, bf16[6,256,256]{2,1,0:T(8,128)(2,1)} %constant.11.clone.turn_hbm, ...), custom_call_target="tpu_custom_call" | custom-call | tf_op jit(solution)/shard_map/hamiltonian/pallas_call | solution.py:435
  75.6 0.8 %copy.13 = f32[2,1,4,128,128]{4,3,2,1,0:T(8,128)} copy(f32[2,1,4,128,128]{4,3,2,1,0:T(8,128)S(1)} %hamiltonian.1) | data formatting | bytes 1048576
